TPU v7x, 512 devices: a whole 4x8x8 slice. The times are simulated.
512 devices in a mesh: level: 16 (over x_lo, y), seq: 32 (over z, x_hi, core).
Axes of the slice: x: 4 (x_hi: 2, x_lo: 2; x = x_hi * 2 + x_lo), y: 8, z: 8, core: 2. Of those that a mesh axis runs over, the one named last changes fastest.
Arguments:
- queries: bfloat16 [16, 8192, 1536], P('level', 'seq'), may hold values from -9 to 9
- keys: bfloat16 [16, 8192, 1536], P('level', 'seq'), may hold values from -9 to 9
- values: bfloat16 [16, 8192, 1536], P('level', 'seq'), may hold values from -6 to 6
- state: bfloat16 [16, 8192, 1536], P('level', 'seq'), may hold values from -6 to 6
- timestep: int32 [16], P('level'), may hold values from 1 to 16
- gate_table: bfloat16 [16, 1536], replicated, may hold values from -4 to 4
Outputs:
- velocity: bfloat16 [16, 8192, 1536], P('level', 'seq')
- advanced: bfloat16 [16, 8192, 1536], P('level', 'seq')
All inputs are finite; a program needn't handle non-finite values.
Results may differ from a plain program's by a relative error of at most 0.0051.
Values may be sent and summed in bfloat16 or wider, within the bound.
A program may use at most 64 MiB of HBM per device.

v0:
```python
import math

import jax
import jax.numpy as jnp
from jax import lax
from jax.sharding import PartitionSpec as P

HEADS = 12
HEAD_DIM = 128
REACH = 2
STEPS = 16


PAIRED = 2
FLOOR_VALUE = -1e30


def passed_along(block, axis, distance):
    devices = range(lax.axis_size(axis))
    route = [(i - distance, i) for i in devices if i - distance in devices]
    return lax.ppermute(block, axis, route)


def passed_along_2(value, axis, steps):
    count = lax.axis_size(axis)
    pairs = [(source, (source + steps) % count) for source in range(count)]
    return lax.ppermute(value, axis, pairs)


def block_parts(query_rows, key_blocks, value_blocks):
    query_count = query_rows.shape[0]
    block_count = key_blocks.shape[0]
    block_width = key_blocks.shape[1]
    group_count = HEADS // PAIRED
    query_groups = jnp.moveaxis(
        query_rows.reshape(query_count, group_count, PAIRED, HEAD_DIM), 1, 0
    )
    key_groups = jnp.moveaxis(
        key_blocks.reshape(block_count, block_width, group_count, PAIRED, HEAD_DIM), 2, 0
    )
    value_groups = jnp.moveaxis(
        value_blocks.reshape(block_count, block_width, group_count, PAIRED, HEAD_DIM), 2, 0
    )
    scaling = 1.0 / math.sqrt(HEAD_DIM)

    def one_group(operands):
        query_part, key_part, value_part = operands
        scores = (
            jnp.einsum("qhe,cshe->chqs", query_part, key_part, preferred_element_type=jnp.float32)
            * scaling
        )
        highest = jnp.max(scores, axis=-1)
        weights = jnp.exp(scores - highest[..., None])
        totals = jnp.sum(weights, axis=-1)
        rounded = weights.astype(jnp.bfloat16)
        blended = jnp.einsum(
            "chqs,cshe->cqhe", rounded, value_part, preferred_element_type=jnp.float32
        )
        partial_out = (blended / jnp.moveaxis(totals, 1, 2)[..., None]).astype(jnp.bfloat16)
        return (partial_out, highest + jnp.log(totals))

    partial_out, log_totals = lax.map(one_group, (query_groups, key_groups, value_groups))
    partial_out = jnp.moveaxis(partial_out, 0, 2).reshape(
        block_count, query_count, HEADS * HEAD_DIM
    )
    log_totals = jnp.moveaxis(log_totals, 0, 1).reshape(block_count, HEADS, query_count)
    return (partial_out, log_totals)


def merge_parts(partial_out, log_totals, usable):
    masked = jnp.where(usable[:, None, None], log_totals, FLOOR_VALUE)
    highest = jnp.max(masked, axis=0)
    weights = jnp.exp(masked - highest[None])
    totals = jnp.sum(weights, axis=0)
    block_count = partial_out.shape[0]
    query_count = partial_out.shape[1]
    split_out = partial_out.reshape(block_count, query_count, HEADS, HEAD_DIM)
    summed = jnp.einsum("cqhe,chq->qhe", split_out, weights, preferred_element_type=jnp.float32)
    return (summed / jnp.moveaxis(totals, 0, 1)[..., None]).reshape(query_count, HEADS * HEAD_DIM)


def on_device(queries, keys, values, state, timestep, gate_table):
    axis_count = lax.axis_size("seq")
    position = lax.axis_index("seq")
    offsets = []
    for distance in range(1, REACH + 1):
        offsets = offsets + [distance, -distance]
    key_list = [keys[0]]
    value_list = [values[0]]
    nearby = [position]
    for shift_by in offsets:
        moved_keys, moved_values = passed_along((keys, values), "seq", shift_by)
        key_list.append(moved_keys[0])
        value_list.append(moved_values[0])
        nearby.append(position - shift_by)
    merged_out, merged_total = block_parts(queries[0], jnp.stack(key_list), jnp.stack(value_list))
    nearby_blocks = jnp.stack(nearby)
    usable = (nearby_blocks >= 0) & (nearby_blocks < axis_count)
    attended = merge_parts(merged_out, merged_total, usable)
    selector = (jnp.arange(1, gate_table.shape[0] + 1, dtype=jnp.int32) == timestep[0]).astype(
        jnp.bfloat16
    )
    gate_row = jnp.dot(selector[None, :], gate_table, preferred_element_type=jnp.float32)
    velocity = (gate_row * attended).astype(jnp.bfloat16)
    factor = -(2.0 * timestep[0].astype(jnp.float32) - 1.0) / (STEPS * STEPS)
    updated = (state[0].astype(jnp.float32) + factor * velocity.astype(jnp.float32)).astype(
        jnp.bfloat16
    )
    advanced = passed_along_2(updated[None], "level", -1)
    return (velocity[None], advanced)


def solution(mesh):
    placed = (
        P("level", "seq", None),
        P("level", "seq", None),
        P("level", "seq", None),
        P("level", "seq", None),
        P("level"),
        P(),
    )
    return jax.shard_map(
        on_device,
        mesh=mesh,
        in_specs=placed,
        out_specs=(P("level", "seq", None), P("level", "seq", None)),
        check_vma=False,
    )
```

profile of v0, /device:TPU:318, one launch (start us, length us, event | category | flops | bytes accessed | tf_op | source)
XLA Modules:
  0.0 175.5 jit_solution(7299564665780443496)
XLA Ops:
  0.7 1.5 copy.16
  2.1 1.9 %collective-permute-start = (bf16[1,256,1536]{1,2,0:T(8,128)(2,1)S(1)}, bf16[1,256,1536]{1,2,0:T(8,128)(2,1)}, u32[]{:S(2)}, u32[]{:S(2)}) collective-permute-start(bf16[1,256,1536]{1,2,0:T(8,128)(2,1)S(1)} %copy.16), channel_id=1, source_target_pairs={{0,1},{1,2},{2,3},{3,4},{4,5},{5,6},{6,7},{7,8},{8,9},{9,10},{10,1... | collective-permute-start | bytes 2359304 | tf_op jit(solution)/shard_map/ppermute | solution.py:21
  4.1 5.1 %collective-permute-start.1 = (bf16[1,256,1536]{1,2,0:T(8,128)(2,1)S(1)}, bf16[1,256,1536]{1,2,0:T(8,128)(2,1)}, u32[]{:S(2)}, u32[]{:S(2)}) collective-permute-start(bf16[1,256,1536]{1,2,0:T(8,128)(2,1)S(1)} %copy.16), channel_id=1, source_target_pairs={{1,0},{2,1},{3,2},{4,3},{5,4},{6,5},{7,6},{8,7},{9,8},{10,9},{11,1... | collective-permute-start | bytes 2359304 | tf_op jit(solution)/shard_map/ppermute | solution.py:21
  9.2 5.1 %collective-permute-start.2 = (bf16[1,256,1536]{1,2,0:T(8,128)(2,1)S(1)}, bf16[1,256,1536]{1,2,0:T(8,128)(2,1)}, u32[]{:S(2)}, u32[]{:S(2)}) collective-permute-start(bf16[1,256,1536]{1,2,0:T(8,128)(2,1)S(1)} %copy.16), channel_id=1, source_target_pairs={{0,2},{1,3},{2,4},{3,5},{4,6},{5,7},{6,8},{7,9},{8,10},{9,11},{10,... | collective-permute-start | bytes 2359304 | tf_op jit(solution)/shard_map/ppermute | solution.py:21
  14.4 2.2 %collective-permute-start.3 = (bf16[1,256,1536]{1,2,0:T(8,128)(2,1)S(1)}, bf16[1,256,1536]{1,2,0:T(8,128)(2,1)}, u32[]{:S(2)}, u32[]{:S(2)}) collective-permute-start(bf16[1,256,1536]{1,2,0:T(8,128)(2,1)S(1)} %copy.16), channel_id=1, source_target_pairs={{2,0},{3,1},{4,2},{5,3},{6,4},{7,5},{8,6},{9,7},{10,8},{11,9},{12,... | collective-permute-start | bytes 2359304 | tf_op jit(solution)/shard_map/ppermute | solution.py:21
  18.0 1.9 %collective-permute-start.4 = (bf16[1,256,1536]{1,2,0:T(8,128)(2,1)S(1)}, bf16[1,256,1536]{1,2,0:T(8,128)(2,1)}, u32[]{:S(2)}, u32[]{:S(2)}) collective-permute-start(bf16[1,256,1536]{1,2,0:T(8,128)(2,1)S(1)} %copy.21), channel_id=1, source_target_pairs={{0,1},{1,2},{2,3},{3,4},{4,5},{5,6},{6,7},{7,8},{8,9},{9,10},{10,1... | collective-permute-start | bytes 2359304 | tf_op jit(solution)/shard_map/ppermute | solution.py:21
  23.0 2.3 %copy.27 = bf16[1,256,1536]{1,2,0:T(8,128)(2,1)} copy(bf16[1,256,1536]{2,1,0:T(8,128)(2,1)} %param.11) | data formatting | bytes 1572864 | tf_op args[3]
  25.3 28.3 %collective-permute-done = bf16[1,256,1536]{1,2,0:T(8,128)(2,1)} collective-permute-done((bf16[1,256,1536]{1,2,0:T(8,128)(2,1)S(1)}, bf16[1,256,1536]{1,2,0:T(8,128)(2,1)}, u32[]{:S(2)}, u32[]{:S(2)}) %collective-permute-start) | collective-permute-done | bytes 786464 | tf_op jit(solution)/shard_map/ppermute | solution.py:21
  53.6 1.9 %collective-permute-start.5 = (bf16[1,256,1536]{1,2,0:T(8,128)(2,1)S(1)}, bf16[1,256,1536]{1,2,0:T(8,128)(2,1)S(1)}, u32[]{:S(2)}, u32[]{:S(2)}) collective-permute-start(bf16[1,256,1536]{1,2,0:T(8,128)(2,1)S(1)} %copy.21), channel_id=1, source_target_pairs={{1,0},{2,1},{3,2},{4,3},{5,4},{6,5},{7,6},{8,7},{9,8},{10,9},{11,1... | collective-permute-start | bytes 2359304 | tf_op jit(solution)/shard_map/ppermute | solution.py:21
  55.5 2.2 %constant_dynamic-update-slice_fusion.4 = bf16[5,256,1536]{1,2,0:T(8,128)(2,1)} fusion(bf16[5,256,1536]{1,2,0:T(8,128)(2,1)} %constant_dynamic-update-slice_fusion.5, bf16[1,256,1536]{1,2,0:T(8,128)(2,1)} %collective-permute-done), kind=kLoop, calls=%fused_computation.36 | loop fusion | bytes 1572864
  58.5 1.9 %collective-permute-start.6 = (bf16[1,256,1536]{1,2,0:T(8,128)(2,1)S(1)}, bf16[1,256,1536]{1,2,0:T(8,128)(2,1)S(1)}, u32[]{:S(2)}, u32[]{:S(2)}) collective-permute-start(bf16[1,256,1536]{1,2,0:T(8,128)(2,1)S(1)} %copy.21), channel_id=1, source_target_pairs={{0,2},{1,3},{2,4},{3,5},{4,6},{5,7},{6,8},{7,9},{8,10},{9,11},{10,... | collective-permute-start | bytes 2359304 | tf_op jit(solution)/shard_map/ppermute | solution.py:21
  60.4 2.1 %constant_dynamic-update-slice_fusion.3 = bf16[5,256,1536]{1,2,0:T(8,128)(2,1)} fusion(bf16[5,256,1536]{1,2,0:T(8,128)(2,1)} %constant_dynamic-update-slice_fusion.4, bf16[1,256,1536]{1,2,0:T(8,128)(2,1)} %collective-permute-done.1), kind=kLoop, calls=%fused_computation.35 | loop fusion | bytes 1572864
  62.5 2.3 %collective-permute-done.2 = bf16[1,256,1536]{1,2,0:T(8,128)(2,1)} collective-permute-done((bf16[1,256,1536]{1,2,0:T(8,128)(2,1)S(1)}, bf16[1,256,1536]{1,2,0:T(8,128)(2,1)}, u32[]{:S(2)}, u32[]{:S(2)}) %collective-permute-start.2) | collective-permute-done | bytes 786464 | tf_op jit(solution)/shard_map/ppermute | solution.py:21
  64.8 3.1 %collective-permute-start.7 = (bf16[1,256,1536]{1,2,0:T(8,128)(2,1)S(1)}, bf16[1,256,1536]{1,2,0:T(8,128)(2,1)S(1)}, u32[]{:S(2)}, u32[]{:S(2)}) collective-permute-start(bf16[1,256,1536]{1,2,0:T(8,128)(2,1)S(1)} %copy.21), channel_id=1, source_target_pairs={{2,0},{3,1},{4,2},{5,3},{6,4},{7,5},{8,6},{9,7},{10,8},{11,9},{12,... | collective-permute-start | bytes 2359304 | tf_op jit(solution)/shard_map/ppermute | solution.py:21
  67.9 2.1 %constant_dynamic-update-slice_fusion.2 = bf16[5,256,1536]{1,2,0:T(8,128)(2,1)} fusion(bf16[5,256,1536]{1,2,0:T(8,128)(2,1)} %constant_dynamic-update-slice_fusion.3, bf16[1,256,1536]{1,2,0:T(8,128)(2,1)} %collective-permute-done.2), kind=kLoop, calls=%fused_computation.34 | loop fusion | bytes 1572864
  70.0 21.4 %collective-permute-done.3 = bf16[1,256,1536]{1,2,0:T(8,128)(2,1)} collective-permute-done((bf16[1,256,1536]{1,2,0:T(8,128)(2,1)S(1)}, bf16[1,256,1536]{1,2,0:T(8,128)(2,1)}, u32[]{:S(2)}, u32[]{:S(2)}) %collective-permute-start.3) | collective-permute-done | bytes 786464 | tf_op jit(solution)/shard_map/ppermute | solution.py:21
  91.4 2.1 %constant_dynamic-update-slice_fusion.1 = bf16[5,256,1536]{1,2,0:T(8,128)(2,1)} fusion(bf16[5,256,1536]{1,2,0:T(8,128)(2,1)} %constant_dynamic-update-slice_fusion.2, bf16[1,256,1536]{1,2,0:T(8,128)(2,1)} %collective-permute-done.3), kind=kLoop, calls=%fused_computation.33 | loop fusion | bytes 1572864 | tf_op jit(solution)/shard_map/stack | solution.py:96
  93.5 7.8 %collective-permute-done.4 = bf16[1,256,1536]{1,2,0:T(8,128)(2,1)} collective-permute-done((bf16[1,256,1536]{1,2,0:T(8,128)(2,1)S(1)}, bf16[1,256,1536]{1,2,0:T(8,128)(2,1)}, u32[]{:S(2)}, u32[]{:S(2)}) %collective-permute-start.4) | collective-permute-done | bytes 786464 | tf_op jit(solution)/shard_map/ppermute | solution.py:21
  102.7 6.5 %collective-permute-done.7 = bf16[1,256,1536]{1,2,0:T(8,128)(2,1)S(1)} collective-permute-done((bf16[1,256,1536]{1,2,0:T(8,128)(2,1)S(1)}, bf16[1,256,1536]{1,2,0:T(8,128)(2,1)S(1)}, u32[]{:S(2)}, u32[]{:S(2)}) %collective-permute-start.7) | collective-permute-done | bytes 786464 | tf_op jit(solution)/shard_map/ppermute | solution.py:21
  109.2 1.9 %copy-done.2 = bf16[5,256,1536]{1,2,0:T(8,128)(2,1)} copy-done((bf16[5,256,1536]{1,2,0:T(8,128)(2,1)}, bf16[5,256,1536]{1,2,0:T(8,128)(2,1)S(1)}, u32[]{:S(2)}) %copy-start.2) | copy-done | bytes 3932184
  111.1 31.9 %while.12 = (s32[]{:T(128)}, bf16[6,5,256,2,128]{4,2,3,0,1:T(8,128)(2,1)}, f32[6,5,2,256]{3,1,2,0:T(8,128)S(1)}, bf16[6,5,256,2,128]{2,4,3,0,1:T(8,128)(2,1)}, b...) while((s32[]{:T(128)}, bf16[6,5,256,2,128]{4,2,3,0,1:T(8,128)(2,1)}, ...), condition=%wide.region_3.4_spmd, body=%wide.region_0.3_spmd.sunk | while | flops 340129280 | bytes 15316057 | solution.py:62
  143.4 4.9 %multiply_reduce_fusion = f32[256,12,128]{2,0,1:T(8,128)S(1)} fusion(bf16[256,12,5,128]{3,0,1,2:T(8,128)(2,1)} %bitcast.106, f32[256,12,5]{0,1,2:T(8,128)S(1)} %copy.37), kind=kLoop, calls=%fused_computation.21 | loop fusion | flops 5505024 | bytes 5566464
  150.5 3.3 %collective-permute-start.8 = (bf16[1,256,1536]{1,2,0:T(8,128)(2,1)S(1)}, bf16[1,256,1536]{1,2,0:T(8,128)(2,1)S(1)}, u32[]{:S(2)}, u32[]{:S(2)}) collective-permute-start(bf16[1,256,1536]{1,2,0:T(8,128)(2,1)S(1)} %get-tuple-element.57), channel_id=1, source_target_pairs={{0,480},{32,0},{64,32},{96,64},{128,96},{160,128},{192,160},{224,1... | collective-permute-start | bytes 2359304 | tf_op jit(solution)/shard_map/ppermute | solution.py:27
  154.9 19.4 %collective-permute-done.8 = bf16[1,256,1536]{1,2,0:T(8,128)(2,1)S(1)} collective-permute-done((bf16[1,256,1536]{1,2,0:T(8,128)(2,1)S(1)}, bf16[1,256,1536]{1,2,0:T(8,128)(2,1)S(1)}, u32[]{:S(2)}, u32[]{:S(2)}) %collective-permute-start.8) | collective-permute-done | bytes 786464 | tf_op jit(solution)/shard_map/ppermute | solution.py:27
  (88 shorter events, 42.4 us)
Async XLA Ops:
  0.6 22.0 %copy-start = (bf16[16,1536]{1,0:T(8,128)(2,1)S(1)}, bf16[16,1536]{1,0:T(8,128)(2,1)}, u32[]{:S(2)}) copy-start(bf16[16,1536]{1,0:T(8,128)(2,1)} %param.13) | copy-start | bytes 147460
  0.6 22.1 %copy-start.3 = (bf16[1,256,1536]{2,1,0:T(8,128)(2,1)S(1)}, bf16[1,256,1536]{2,1,0:T(8,128)(2,1)}, u32[]{:S(2)}) copy-start(bf16[1,256,1536]{2,1,0:T(8,128)(2,1)} %param.8) | copy-start | bytes 2359300
  2.1 51.5 %collective-permute-start = (bf16[1,256,1536]{1,2,0:T(8,128)(2,1)S(1)}, bf16[1,256,1536]{1,2,0:T(8,128)(2,1)}, u32[]{:S(2)}, u32[]{:S(2)}) collective-permute-start(bf16[1,256,1536]{1,2,0:T(8,128)(2,1)S(1)} %copy.16), channel_id=1, source_target_pairs={{0,1},{1,2},{2,3},{3,4},{4,5},{5,6},{6,7},{7,8},{8,9},{9,10},{10,1... | collective-permute-start | bytes 2359304 | tf_op jit(solution)/shard_map/ppermute | solution.py:21
  4.1 54.4 %collective-permute-start.1 = (bf16[1,256,1536]{1,2,0:T(8,128)(2,1)S(1)}, bf16[1,256,1536]{1,2,0:T(8,128)(2,1)}, u32[]{:S(2)}, u32[]{:S(2)}) collective-permute-start(bf16[1,256,1536]{1,2,0:T(8,128)(2,1)S(1)} %copy.16), channel_id=1, source_target_pairs={{1,0},{2,1},{3,2},{4,3},{5,4},{6,5},{7,6},{8,7},{9,8},{10,9},{11,1... | collective-permute-start | bytes 2359304 | tf_op jit(solution)/shard_map/ppermute | solution.py:21
  9.2 55.6 %collective-permute-start.2 = (bf16[1,256,1536]{1,2,0:T(8,128)(2,1)S(1)}, bf16[1,256,1536]{1,2,0:T(8,128)(2,1)}, u32[]{:S(2)}, u32[]{:S(2)}) collective-permute-start(bf16[1,256,1536]{1,2,0:T(8,128)(2,1)S(1)} %copy.16), channel_id=1, source_target_pairs={{0,2},{1,3},{2,4},{3,5},{4,6},{5,7},{6,8},{7,9},{8,10},{9,11},{10,... | collective-permute-start | bytes 2359304 | tf_op jit(solution)/shard_map/ppermute | solution.py:21
  14.4 77.0 %collective-permute-start.3 = (bf16[1,256,1536]{1,2,0:T(8,128)(2,1)S(1)}, bf16[1,256,1536]{1,2,0:T(8,128)(2,1)}, u32[]{:S(2)}, u32[]{:S(2)}) collective-permute-start(bf16[1,256,1536]{1,2,0:T(8,128)(2,1)S(1)} %copy.16), channel_id=1, source_target_pairs={{2,0},{3,1},{4,2},{5,3},{6,4},{7,5},{8,6},{9,7},{10,8},{11,9},{12,... | collective-permute-start | bytes 2359304 | tf_op jit(solution)/shard_map/ppermute | solution.py:21
  18.0 83.3 %collective-permute-start.4 = (bf16[1,256,1536]{1,2,0:T(8,128)(2,1)S(1)}, bf16[1,256,1536]{1,2,0:T(8,128)(2,1)}, u32[]{:S(2)}, u32[]{:S(2)}) collective-permute-start(bf16[1,256,1536]{1,2,0:T(8,128)(2,1)S(1)} %copy.21), channel_id=1, source_target_pairs={{0,1},{1,2},{2,3},{3,4},{4,5},{5,6},{6,7},{7,8},{8,9},{9,10},{10,1... | collective-permute-start | bytes 2359304 | tf_op jit(solution)/shard_map/ppermute | solution.py:21
  25.3 76.0 %copy-start.1 = (bf16[5,256,1536]{1,2,0:T(8,128)(2,1)S(1)}, bf16[5,256,1536]{1,2,0:T(8,128)(2,1)}, u32[]{:S(2)}) copy-start(bf16[5,256,1536]{1,2,0:T(8,128)(2,1)} %constant_dynamic-update-slice_fusion.10) | copy-start | bytes 11796484
  53.6 48.9 %collective-permute-start.5 = (bf16[1,256,1536]{1,2,0:T(8,128)(2,1)S(1)}, bf16[1,256,1536]{1,2,0:T(8,128)(2,1)S(1)}, u32[]{:S(2)}, u32[]{:S(2)}) collective-permute-start(bf16[1,256,1536]{1,2,0:T(8,128)(2,1)S(1)} %copy.21), channel_id=1, source_target_pairs={{1,0},{2,1},{3,2},{4,3},{5,4},{6,5},{7,6},{8,7},{9,8},{10,9},{11,1... | collective-permute-start | bytes 2359304 | tf_op jit(solution)/shard_map/ppermute | solution.py:21
  58.5 44.1 %collective-permute-start.6 = (bf16[1,256,1536]{1,2,0:T(8,128)(2,1)S(1)}, bf16[1,256,1536]{1,2,0:T(8,128)(2,1)S(1)}, u32[]{:S(2)}, u32[]{:S(2)}) collective-permute-start(bf16[1,256,1536]{1,2,0:T(8,128)(2,1)S(1)} %copy.21), channel_id=1, source_target_pairs={{0,2},{1,3},{2,4},{3,5},{4,6},{5,7},{6,8},{7,9},{8,10},{9,11},{10,... | collective-permute-start | bytes 2359304 | tf_op jit(solution)/shard_map/ppermute | solution.py:21
  64.8 44.4 %collective-permute-start.7 = (bf16[1,256,1536]{1,2,0:T(8,128)(2,1)S(1)}, bf16[1,256,1536]{1,2,0:T(8,128)(2,1)S(1)}, u32[]{:S(2)}, u32[]{:S(2)}) collective-permute-start(bf16[1,256,1536]{1,2,0:T(8,128)(2,1)S(1)} %copy.21), channel_id=1, source_target_pairs={{2,0},{3,1},{4,2},{5,3},{6,4},{7,5},{8,6},{9,7},{10,8},{11,9},{12,... | collective-permute-start | bytes 2359304 | tf_op jit(solution)/shard_map/ppermute | solution.py:21
  109.2 1.9 %copy-start.2 = (bf16[5,256,1536]{1,2,0:T(8,128)(2,1)}, bf16[5,256,1536]{1,2,0:T(8,128)(2,1)S(1)}, u32[]{:S(2)}) copy-start(bf16[5,256,1536]{1,2,0:T(8,128)(2,1)S(1)} %constant_dynamic-update-slice_fusion.6) | copy-start | bytes 11796484
  150.5 23.8 %collective-permute-start.8 = (bf16[1,256,1536]{1,2,0:T(8,128)(2,1)S(1)}, bf16[1,256,1536]{1,2,0:T(8,128)(2,1)S(1)}, u32[]{:S(2)}, u32[]{:S(2)}) collective-permute-start(bf16[1,256,1536]{1,2,0:T(8,128)(2,1)S(1)} %get-tuple-element.57), channel_id=1, source_target_pairs={{0,480},{32,0},{64,32},{96,64},{128,96},{160,128},{192,160},{224,1... | collective-permute-start | bytes 2359304 | tf_op jit(solution)/shard_map/ppermute | solution.py:27
where the time goes:
time: 177 us; the launch traced here: 175 us
  waiting for transfers between devices  86.5 us (49%)
  local copies, waits for them, and re-layouts  38.5 us (22%)
  starting transfers between devices  26.6 us (15%)
  matrix products  11.9 us (7%)
  other arithmetic  10.2 us (6%)
    ppermute x8, waiting for transfers between devices, passed_along(): return lax.ppermute(block, axis, route)  67.1 us
    ppermute x8, starting transfers between devices, passed_along(): return lax.ppermute(block, axis, route)  23.3 us
    ppermute x1, waiting for transfers between devices, passed_along_2(): return lax.ppermute(value, axis, pairs)  19.4 us
    unnamed x23, local copies, waits for them, and re-layouts  19.2 us
    dynamic_slice x12, local copies, waits for them, and re-layouts, block_parts(): lax.map(one_group, (query_groups, key_groups, value_groups))  8.75 us
    dot_general x6, matrix products, one_group(): jnp.einsum('chqs,cshe->cqhe', rounded, value_part, preferred_element_type...  8.72 us
    dynamic_update_slice x12, local copies, waits for them, and re-layouts, block_parts(): lax.map(one_group, (query_groups, key_groups, value_groups))  7.74 us
    unnamed x1, other arithmetic  4.94 us
  transfers between devices with their start and end apart: 9, of which 7 were waited for; matrix products, arithmetic and copies ran while one was open for 10% of the time, Pallas kernels for 0%

commit v1 on v0

v1 whole, which is shorter than its diff:
```python
import math

import jax
import jax.numpy as jnp
from jax import lax
from jax.experimental import pallas as pl
from jax.experimental.pallas import tpu as pltpu
from jax.sharding import PartitionSpec as P

HEADS = 12
HEAD_DIM = 128
STEPS = 16
TOK = 256
N_LEVEL = 16
N_Y = 8
N_Z = 8
WINDOW = 3
LAG_PASS = 2
LAG_COMPUTE = 3
MESH = pl.DeviceIdType.MESH
OWN, SIB, ACROSS, ALONG, SHARED = range(5)
FLOOR_VALUE = -1e30


def columns(ref, head):
    return ref.at[:, pl.ds(pl.multiple_of(head * HEAD_DIM, HEAD_DIM), HEAD_DIM)]


def kernel(
    ts_ref, gate_ref, q_hbm, k_hbm, v_hbm, s_hbm, vel_hbm, adv_hbm,
    kv, qs, ss, vel, upd, gates,
    sem_k, sem_v, sem_q, sem_s, sem_vel,
    send_sib, recv_sib, send_x, recv_x, send_z, recv_z, send_d, recv_d, send_l, recv_l,
):
    level = lax.axis_index("level")
    seq = lax.axis_index("seq")
    core = seq % 2
    x_hi = (seq // 2) % 2
    z = seq // 4

    def at(z_, x_hi_, core_):
        return (level, z_ * 4 + x_hi_ * 2 + core_)

    sibling = at(z, x_hi, 1 - core)
    across = at(z, 1 - x_hi, core)
    along_to = at((z + 1 + (N_Z - 2) * x_hi) % N_Z, x_hi, core)
    along_from = at((z + N_Z - 1 - (N_Z - 2) * x_hi) % N_Z, x_hi, core)
    level_to = ((level + N_LEVEL - 1) % N_LEVEL, seq)
    level_from = ((level + 1) % N_LEVEL, seq)

    def load_k(h):
        return pltpu.make_async_copy(columns(k_hbm, h), kv.at[OWN, h, 0], sem_k.at[h])

    def load_v(h):
        return pltpu.make_async_copy(columns(v_hbm, h), kv.at[OWN, h, 1], sem_v.at[h])

    def load_q(h):
        return pltpu.make_async_copy(columns(q_hbm, h), qs.at[h], sem_q.at[h])

    def load_s(h):
        return pltpu.make_async_copy(columns(s_hbm, h), ss.at[h], sem_s.at[h])

    def store_vel(h):
        return pltpu.make_async_copy(vel.at[h], columns(vel_hbm, h), sem_vel.at[h])

    def remote(source, target, send, recv, h, device):
        return pltpu.make_async_remote_copy(
            source, target, send.at[h], recv.at[h], device_id=device, device_id_type=MESH
        )

    def to_sibling(h):
        return remote(kv.at[OWN, h], kv.at[SIB, h], send_sib, recv_sib, h, sibling)

    def to_across(h):
        return remote(kv.at[OWN, h], kv.at[ACROSS, h], send_x, recv_x, h, across)

    def to_along(h):
        return remote(kv.at[ACROSS, h], kv.at[ALONG, h], send_z, recv_z, h, along_to)

    def share_across(h):
        return remote(kv.at[ACROSS, h], kv.at[SHARED, h], send_d, recv_d, h, sibling)

    def share_along(h):
        return remote(kv.at[ALONG, h], kv.at[SHARED, h], send_d, recv_d, h, sibling)

    def to_level(h):
        return remote(upd.at[h], columns(adv_hbm, h), send_l, recv_l, h, level_to)

    for h in range(HEADS):
        load_k(h).start()
        load_v(h).start()
    for h in range(HEADS):
        load_q(h).start()
        load_s(h).start()

    barrier = pltpu.get_barrier_semaphore()
    for device in (sibling, across, along_from, level_from):
        pl.semaphore_signal(barrier, inc=1, device_id=device, device_id_type=MESH)

    step_index = ts_ref[0]
    chosen = lax.broadcasted_iota(jnp.int32, (STEPS, HEADS * HEAD_DIM), 0) == step_index - 1
    gate_row = jnp.sum(
        jnp.where(chosen, gate_ref[...].astype(jnp.float32), 0.0), axis=0, keepdims=True
    )
    for h in range(HEADS):
        gates[h] = jnp.broadcast_to(gate_row[:, h * HEAD_DIM : (h + 1) * HEAD_DIM], (8, HEAD_DIM))
    factor = -(2.0 * step_index.astype(jnp.float32) - 1.0) / (STEPS * STEPS)

    pl.semaphore_wait(barrier, 4)

    def send_own(h):
        load_k(h).wait()
        load_v(h).wait()
        to_across(h).start()
        to_sibling(h).start()

    for h in range(WINDOW):
        send_own(h)

    end = ((z == 0) & (x_hi == 0)) | ((z == N_Z - 1) & (x_hi == 1))
    shares_across = core == x_hi
    bias_along = jnp.where(end, FLOOR_VALUE, 0.0)
    bias_shared = jnp.where(end & shares_across, FLOOR_VALUE, 0.0)
    scaling = math.log2(math.e) / math.sqrt(HEAD_DIM)

    def compute(h):
        load_q(h).wait()
        load_s(h).wait()
        query = qs[h]
        scores = []
        for slot in range(5):
            part = (
                lax.dot_general(
                    query, kv[slot, h, 0], (((1,), (1,)), ((), ())),
                    preferred_element_type=jnp.float32,
                )
                * scaling
            )
            if slot == ALONG:
                part = part + bias_along
            if slot == SHARED:
                part = part + bias_shared
            scores.append(part)
        top = scores[0]
        for part in scores[1:]:
            top = jnp.maximum(top, part)
        top = jnp.max(top, axis=-1, keepdims=True)
        total = None
        blended = None
        for slot in range(5):
            weights = jnp.exp2(scores[slot] - top)
            total = weights if total is None else total + weights
            product = jnp.dot(
                weights.astype(jnp.bfloat16), kv[slot, h, 1], preferred_element_type=jnp.float32
            )
            blended = product if blended is None else blended + product
        attended = blended / jnp.sum(total, axis=-1, keepdims=True)
        velocity = (gates[h][0:1] * attended).astype(jnp.bfloat16)
        vel[h] = velocity
        upd[h] = (ss[h].astype(jnp.float32) + factor * velocity.astype(jnp.float32)).astype(
            jnp.bfloat16
        )
        store_vel(h).start()
        to_level(h).start()

    def step(t, carry):
        @pl.when(t < HEADS)
        def _():
            to_across(t).wait_recv()
            to_along(t).start()

            @pl.when(shares_across)
            def _():
                share_across(t).start()

            @pl.when(t + WINDOW < HEADS)
            def _():
                send_own(t + WINDOW)

        @pl.when((t >= LAG_PASS) & (t < LAG_PASS + HEADS))
        def _():
            to_along(t - LAG_PASS).wait_recv()

            @pl.when(jnp.logical_not(shares_across))
            def _():
                share_along(t - LAG_PASS).start()

        @pl.when(t >= LAG_COMPUTE)
        def _():
            h = t - LAG_COMPUTE
            to_sibling(h).wait_recv()
            share_across(h).wait_recv()
            compute(h)

        return carry

    lax.fori_loop(0, HEADS + LAG_COMPUTE, step, 0)

    def drain(h, carry):
        to_sibling(h).wait_send()
        to_across(h).wait_send()
        to_along(h).wait_send()
        share_across(h).wait_send()
        store_vel(h).wait()
        to_level(h).wait_send()
        to_level(h).wait_recv()
        return carry

    lax.fori_loop(0, HEADS, drain, 0)


def on_device(queries, keys, values, state, timestep, gate_table):
    width = HEADS * HEAD_DIM
    anywhere = pl.BlockSpec(memory_space=pltpu.HBM)
    block = jax.ShapeDtypeStruct((TOK, width), jnp.bfloat16)
    heads = (HEADS, TOK, HEAD_DIM)
    velocity, advanced = pl.pallas_call(
        kernel,
        out_shape=(block, block),
        in_specs=[
            pl.BlockSpec(memory_space=pltpu.SMEM),
            pl.BlockSpec(memory_space=pltpu.VMEM),
            anywhere, anywhere, anywhere, anywhere,
        ],
        out_specs=(anywhere, anywhere),
        scratch_shapes=[
            pltpu.VMEM((5, HEADS, 2, TOK, HEAD_DIM), jnp.bfloat16),
            pltpu.VMEM(heads, jnp.bfloat16),
            pltpu.VMEM(heads, jnp.bfloat16),
            pltpu.VMEM(heads, jnp.bfloat16),
            pltpu.VMEM(heads, jnp.bfloat16),
            pltpu.VMEM((HEADS, 8, HEAD_DIM), jnp.float32),
        ]
        + [pltpu.SemaphoreType.DMA((HEADS,))] * 15,
        compiler_params=pltpu.CompilerParams(
            collective_id=0, has_side_effects=True, vmem_limit_bytes=60 << 20
        ),
        name="window_attention",
    )(timestep, gate_table, queries[0], keys[0], values[0], state[0])
    return (velocity[None], advanced[None])


def solution(mesh):
    placed = (
        P("level", "seq", None),
        P("level", "seq", None),
        P("level", "seq", None),
        P("level", "seq", None),
        P("level"),
        P(),
    )
    return jax.shard_map(
        on_device,
        mesh=mesh,
        in_specs=placed,
        out_specs=(P("level", "seq", None), P("level", "seq", None)),
        check_vma=False,
    )
```

time: 177 us -> 80.9 us (0.46)
  the two profiles are of different devices: /device:TPU:318 before, /device:TPU:48 now
where the time goes in v1:
time: 80.9 us; the launch traced here: 80.7 us
  Pallas kernels  76.3 us (94%)
  local copies, waits for them, and re-layouts  3.02 us (4%)
  between operations  1.29 us (2%)
    pallas_call x1, Pallas kernels, on_device(): pl.pallas_call(kernel, out_shape=(block, block), in_specs=[pl.BlockSpec(m...  76.3 us
    unnamed x4, local copies, waits for them, and re-layouts  3.02 us

profile of v1, /device:TPU:48, one launch (start us, length us, event | category | flops | bytes accessed | tf_op | source)
XLA Modules:
  0.0 80.7 jit_solution(385441681973875467)
XLA Ops:
  1.3 76.3 %window_attention.1 = (bf16[256,1536]{1,0:T(8,128)(2,1)}, bf16[256,1536]{1,0:T(8,128)(2,1)}) custom-call(s32[1]{0:T(128)S(6)} %copy.10.ts_ref, bf16[16,1536]{1,0:T(8,128)(2,1)} %gate_ref.1, bf16[256,1536]{1,0:T(8,128)(2,1)} %bitcast.8, bf16[256,1536]{1,0:T(8,128)(2,1)} %bitcast.9, bf16[256,1536]{1,0:T(8,128)(2,1)} %bitcast.10, bf16[256,1536]{1,0:T(8,128)(2,1)} %bitcast.11), custom_call_target="tpu_custom_call" | custom-call | tf_op jit(solution)/shard_map/window_attention/pallas_call | solution.py:217
  77.6 0.0 copy-start
  77.6 2.1 %copy.11 = bf16[1,256,1536]{2,1,0:T(8,128)(2,1)} copy(bf16[1,256,1536]{2,1,0:T(8,128)(2,1)} %bitcast.7) | data formatting | bytes 1572864
  79.8 0.0 copy-done
  79.8 0.9 %copy.12 = bf16[1,256,1536]{2,1,0:T(8,128)(2,1)} copy(bf16[1,256,1536]{2,1,0:T(8,128)(2,1)S(1)} %bitcast.6) | data formatting | bytes 1572864
Async XLA Ops:
  77.6 2.1 %copy-start = (bf16[256,1536]{1,0:T(8,128)(2,1)S(1)}, bf16[256,1536]{1,0:T(8,128)(2,1)}, u32[]{:S(2)}) copy-start(bf16[256,1536]{1,0:T(8,128)(2,1)} %get-tuple-element.5) | copy-start | bytes 2359300

commit v2 on v1

v2 whole, which is shorter than its diff:
```python
import math

import jax
import jax.numpy as jnp
from jax import lax
from jax.experimental import pallas as pl
from jax.experimental.pallas import tpu as pltpu
from jax.sharding import PartitionSpec as P

HEADS = 12
HEAD_DIM = 128
STEPS = 16
TOK = 256
N_LEVEL = 16
N_Y = 8
N_Z = 8
WINDOW = 3
LAG_COMPUTE = 2
LAG_RELAY = 3
RELAYED = N_Y - 1
MESH = pl.DeviceIdType.MESH
OWN, SIB, ACROSS, ALONG, SHARED = range(5)
FLOOR_VALUE = -1e30


def columns(ref, head):
    return ref.at[:, pl.ds(pl.multiple_of(head * HEAD_DIM, HEAD_DIM), HEAD_DIM)]


def kernel(
    ts_ref, gate_hbm, q_hbm, k_hbm, v_hbm, s_hbm, vel_hbm, adv_hbm,
    kv, qs, ss, vel, upd, gate_table, gates, relay,
    sem_own, send_sib, recv_sib, send_x, recv_x, send_z, recv_z, send_d, recv_d,
    sem_q, sem_s, sem_vel, send_l, recv_l, sem_gate, send_r, recv_r,
):
    level = lax.axis_index("level")
    seq = lax.axis_index("seq")
    core = seq % 2
    x_hi = (seq // 2) % 2
    z = seq // 4
    x_lo = level // N_Y
    y = level % N_Y

    def at(z_, x_hi_, core_):
        return (level, z_ * 4 + x_hi_ * 2 + core_)

    def on_level(x_lo_, y_):
        return (x_lo_ * N_Y + y_, seq)

    sibling = at(z, x_hi, 1 - core)
    across = at(z, 1 - x_hi, core)
    along_to = at((z + 1 + (N_Z - 2) * x_hi) % N_Z, x_hi, core)
    along_from = at((z + N_Z - 1 - (N_Z - 2) * x_hi) % N_Z, x_hi, core)
    level_to = ((level + N_LEVEL - 1) % N_LEVEL, seq)
    end = ((z == 0) & (x_hi == 0)) | ((z == N_Z - 1) & (x_hi == 1))
    passes = jnp.logical_not(((z == 0) & (x_hi == 1)) | ((z == N_Z - 1) & (x_hi == 0)))
    shares_across = core == x_hi

    barrier = pltpu.get_barrier_semaphore()

    def greet(device):
        pl.semaphore_signal(barrier, inc=1, device_id=device, device_id_type=MESH)

    greet(across)
    greet(sibling)

    @pl.when(jnp.logical_not(end))
    def _():
        greet(along_from)

    greet(on_level(1 - x_lo, 0))

    @pl.when(y < RELAYED)
    def _():
        greet(on_level(x_lo, y + 1))

    @pl.when(y == RELAYED)
    def _():
        for row in range(RELAYED):
            greet(on_level(x_lo, row))

    def load_gate():
        return pltpu.make_async_copy(gate_hbm, gate_table, sem_gate)

    def own_part(h, kind):
        return columns(v_hbm if kind else k_hbm, h)

    def load_own(h, kind):
        u = 2 * h + kind
        return pltpu.make_async_copy(own_part(h, kind), kv.at[OWN, u], sem_own.at[u])

    def load_q(h):
        return pltpu.make_async_copy(columns(q_hbm, h), qs.at[h], sem_q.at[h])

    def load_s(h):
        return pltpu.make_async_copy(columns(s_hbm, h), ss.at[h], sem_s.at[h])

    def store_vel(h):
        return pltpu.make_async_copy(vel.at[h], columns(vel_hbm, h), sem_vel.at[h])

    def remote(source, target, send, recv, device):
        return pltpu.make_async_remote_copy(
            source, target, send, recv, device_id=device, device_id_type=MESH
        )

    def to_sibling(h, kind):
        u = 2 * h + kind
        return remote(kv.at[OWN, u], kv.at[SIB, u], send_sib.at[u], recv_sib.at[u], sibling)

    def to_across(h, kind):
        u = 2 * h + kind
        return remote(kv.at[OWN, u], kv.at[ACROSS, u], send_x.at[u], recv_x.at[u], across)

    def to_along(u):
        return remote(kv.at[ACROSS, u], kv.at[ALONG, u], send_z.at[u], recv_z.at[u], along_to)

    def own_as_along(u):
        return pltpu.make_async_copy(kv.at[OWN, u], kv.at[ALONG, u], recv_z.at[u])

    def share(slot, u):
        return remote(kv.at[slot, u], kv.at[SHARED, u], send_d.at[u], recv_d.at[u], sibling)

    def to_level(h):
        return remote(upd.at[h], columns(adv_hbm, h), send_l.at[h], recv_l.at[h], level_to)

    def to_relay(h):
        return remote(upd.at[h], relay, send_l.at[h], recv_r, on_level(1 - x_lo, h))

    def from_relay():
        return remote(relay, columns(adv_hbm, y), send_r, recv_l.at[y], on_level(x_lo, RELAYED))

    def send_own(h):
        for kind in range(2):
            load_own(h, kind).wait()
        for kind in range(2):
            to_across(h, kind).start()
        for kind in range(2):
            to_sibling(h, kind).start()

    def load_rest(h):
        load_q(h).start()
        load_s(h).start()

    for h in range(HEADS):
        for kind in range(2):
            load_own(h, kind).start()
    load_gate().start()
    count = 2 + passes.astype(jnp.int32) + 1 + (y < RELAYED).astype(jnp.int32)
    count = count + RELAYED * (y == 0).astype(jnp.int32)
    pl.semaphore_wait(barrier, count)
    for h in range(WINDOW):
        send_own(h)
    for h in range(WINDOW):
        load_rest(h)

    load_gate().wait()
    step_index = ts_ref[0]
    chosen = lax.broadcasted_iota(jnp.int32, (STEPS, HEADS * HEAD_DIM), 0) == step_index - 1
    gate_row = jnp.sum(
        jnp.where(chosen, gate_table[...].astype(jnp.float32), 0.0), axis=0, keepdims=True
    )
    for h in range(HEADS):
        gates[h] = jnp.broadcast_to(gate_row[:, h * HEAD_DIM : (h + 1) * HEAD_DIM], (8, HEAD_DIM))
    factor = -(2.0 * step_index.astype(jnp.float32) - 1.0) / (STEPS * STEPS)

    bias_along = jnp.where(end, FLOOR_VALUE, 0.0)
    bias_shared = jnp.where(end & shares_across, FLOOR_VALUE, 0.0)
    scaling = math.log2(math.e) / math.sqrt(HEAD_DIM)

    def compute(h):
        query = qs[h]
        scores = []
        for slot in range(5):
            part = (
                lax.dot_general(
                    query, kv[slot, 2 * h], (((1,), (1,)), ((), ())),
                    preferred_element_type=jnp.float32,
                )
                * scaling
            )
            if slot == ALONG:
                part = part + bias_along
            if slot == SHARED:
                part = part + bias_shared
            scores.append(part)
        top = scores[0]
        for part in scores[1:]:
            top = jnp.maximum(top, part)
        top = jnp.max(top, axis=-1, keepdims=True)
        total = None
        blended = None
        for slot in range(5):
            weights = jnp.exp2(scores[slot] - top)
            total = weights if total is None else total + weights
            product = jnp.dot(
                weights.astype(jnp.bfloat16), kv[slot, 2 * h + 1],
                preferred_element_type=jnp.float32,
            )
            blended = product if blended is None else blended + product
        attended = blended / jnp.sum(total, axis=-1, keepdims=True)
        velocity = (gates[h][0:1] * attended).astype(jnp.bfloat16)
        vel[h] = velocity
        upd[h] = (ss[h].astype(jnp.float32) + factor * velocity.astype(jnp.float32)).astype(
            jnp.bfloat16
        )

    def step(t, carry):
        for kind in range(2):

            @pl.when(t < HEADS)
            def _():
                u = 2 * t + kind
                to_across(t, kind).wait_recv()

                @pl.when(passes)
                def _():
                    to_along(u).start()

                @pl.when(shares_across)
                def _():
                    share(ACROSS, u).start()

            @pl.when((t >= 1) & (t <= HEADS))
            def _():
                u = 2 * t - 2 + kind

                @pl.when(end)
                def _():
                    own_as_along(u).start()

                to_along(u).wait_recv()

                @pl.when(jnp.logical_not(shares_across))
                def _():
                    share(ALONG, u).start()

        @pl.when(t + WINDOW < HEADS)
        def _():
            send_own(t + WINDOW)
            load_rest(t + WINDOW)

        @pl.when(t >= LAG_COMPUTE)
        def _():
            h = t - LAG_COMPUTE
            for kind in range(2):
                to_sibling(h, kind).wait_recv()
                share(ACROSS, 2 * h + kind).wait_recv()
            load_q(h).wait()
            load_s(h).wait()
            compute(h)

            @pl.when((y == 0) & (h < RELAYED))
            def _():
                to_relay(h).start()

            @pl.when((y > 0) | (h >= RELAYED))
            def _():
                to_level(h).start()

            store_vel(h).start()

        @pl.when((y < RELAYED) & (t == y + LAG_COMPUTE + LAG_RELAY))
        def _():
            to_relay(y).wait_recv()
            from_relay().start()

        return carry

    lax.fori_loop(0, HEADS + LAG_COMPUTE, step, 0)

    def drain(h, carry):
        for kind in range(2):
            u = 2 * h + kind
            to_sibling(h, kind).wait_send()
            to_across(h, kind).wait_send()

            @pl.when(passes)
            def _():
                to_along(u).wait_send()

            share(ACROSS, u).wait_send()
        store_vel(h).wait()
        to_level(h).wait_send()
        to_level(h).wait_recv()
        return carry

    lax.fori_loop(0, HEADS, drain, 0)

    @pl.when(y < RELAYED)
    def _():
        from_relay().wait_send()


def on_device(queries, keys, values, state, timestep, gate_table):
    width = HEADS * HEAD_DIM
    anywhere = pl.BlockSpec(memory_space=pltpu.HBM)
    block = jax.ShapeDtypeStruct((TOK, width), jnp.bfloat16)
    heads = (HEADS, TOK, HEAD_DIM)
    velocity, advanced = pl.pallas_call(
        kernel,
        out_shape=(block, block),
        in_specs=[
            pl.BlockSpec(memory_space=pltpu.SMEM),
            anywhere, anywhere, anywhere, anywhere, anywhere,
        ],
        out_specs=(anywhere, anywhere),
        scratch_shapes=[
            pltpu.VMEM((5, 2 * HEADS, TOK, HEAD_DIM), jnp.bfloat16),
            pltpu.VMEM(heads, jnp.bfloat16),
            pltpu.VMEM(heads, jnp.bfloat16),
            pltpu.VMEM(heads, jnp.bfloat16),
            pltpu.VMEM(heads, jnp.bfloat16),
            pltpu.VMEM((STEPS, width), jnp.bfloat16),
            pltpu.VMEM((HEADS, 8, HEAD_DIM), jnp.float32),
            pltpu.VMEM((TOK, HEAD_DIM), jnp.bfloat16),
        ]
        + [pltpu.SemaphoreType.DMA((2 * HEADS,))] * 9
        + [pltpu.SemaphoreType.DMA((HEADS,))] * 5
        + [pltpu.SemaphoreType.DMA] * 3,
        compiler_params=pltpu.CompilerParams(
            collective_id=0, has_side_effects=True, vmem_limit_bytes=60 << 20
        ),
        name="window_attention",
    )(timestep, gate_table, queries[0], keys[0], values[0], state[0])
    return (velocity[None], advanced[None])


def solution(mesh):
    placed = (
        P("level", "seq", None),
        P("level", "seq", None),
        P("level", "seq", None),
        P("level", "seq", None),
        P("level"),
        P(),
    )
    return jax.shard_map(
        on_device,
        mesh=mesh,
        in_specs=placed,
        out_specs=(P("level", "seq", None), P("level", "seq", None)),
        check_vma=False,
    )
```

time: 80.9 us -> 66.6 us (0.82)
  the two profiles are of different devices: /device:TPU:48 before, /device:TPU:61 now
where the time goes in v2:
time: 66.6 us; the launch traced here: 66.4 us
  Pallas kernels  62.1 us (93%)
  local copies, waits for them, and re-layouts  3.02 us (5%)
  between operations  1.29 us (2%)
    pallas_call x1, Pallas kernels, on_device(): pl.pallas_call(kernel, out_shape=(block, block), in_specs=[pl.BlockSpec(m...  62.1 us
    unnamed x4, local copies, waits for them, and re-layouts  3.02 us

profile of v2, /device:TPU:61, one launch (start us, length us, event | category | flops | bytes accessed | tf_op | source)
XLA Modules:
  0.0 66.4 jit_solution(17238558868995120502)
XLA Ops:
  1.3 62.1 %window_attention.1 = (bf16[256,1536]{1,0:T(8,128)(2,1)}, bf16[256,1536]{1,0:T(8,128)(2,1)}) custom-call(s32[1]{0:T(128)S(6)} %copy.10.ts_ref, bf16[16,1536]{1,0:T(8,128)(2,1)} %gate_hbm.1, bf16[256,1536]{1,0:T(8,128)(2,1)} %bitcast.8, bf16[256,1536]{1,0:T(8,128)(2,1)} %bitcast.9, bf16[256,1536]{1,0:T(8,128)(2,1)} %bitcast.10, bf16[256,1536]{1,0:T(8,128)(2,1)} %bitcast.11), custom_call_target="tpu_custom_call" | custom-call | tf_op jit(solution)/shard_map/window_attention/pallas_call | solution.py:299
  63.4 0.0 copy-start
  63.4 2.1 %copy.11 = bf16[1,256,1536]{2,1,0:T(8,128)(2,1)} copy(bf16[1,256,1536]{2,1,0:T(8,128)(2,1)} %bitcast.7) | data formatting | bytes 1572864
  65.5 0.0 copy-done
  65.5 0.9 %copy.12 = bf16[1,256,1536]{2,1,0:T(8,128)(2,1)} copy(bf16[1,256,1536]{2,1,0:T(8,128)(2,1)S(1)} %bitcast.6) | data formatting | bytes 1572864
Async XLA Ops:
  63.4 2.1 %copy-start = (bf16[256,1536]{1,0:T(8,128)(2,1)S(1)}, bf16[256,1536]{1,0:T(8,128)(2,1)}, u32[]{:S(2)}) copy-start(bf16[256,1536]{1,0:T(8,128)(2,1)} %get-tuple-element.5) | copy-start | bytes 2359300

commit v3 on v2

--- a/solution.py
+++ b/solution.py
@@ -15,6 +15,8 @@
 N_Y = 8
 N_Z = 8
 WINDOW = 3
+PIECES = 2
+LAG_PASS = 2
 LAG_COMPUTE = 2
 LAG_RELAY = 3
 RELAYED = N_Y - 1
@@ -31,7 +33,7 @@
     ts_ref, gate_hbm, q_hbm, k_hbm, v_hbm, s_hbm, vel_hbm, adv_hbm,
     kv, qs, ss, vel, upd, gate_table, gates, relay,
     sem_own, send_sib, recv_sib, send_x, recv_x, send_z, recv_z, send_d, recv_d,
-    sem_q, sem_s, sem_vel, send_l, recv_l, sem_gate, send_r, recv_r,
+    sem_q, sem_s, sem_vel, send_l, recv_l, sem_gate, send_r, recv_r, along_ready, level_ready,
 ):
     level = lax.axis_index("level")
     seq = lax.axis_index("seq")
@@ -50,7 +52,6 @@
     sibling = at(z, x_hi, 1 - core)
     across = at(z, 1 - x_hi, core)
     along_to = at((z + 1 + (N_Z - 2) * x_hi) % N_Z, x_hi, core)
-    along_from = at((z + N_Z - 1 - (N_Z - 2) * x_hi) % N_Z, x_hi, core)
     level_to = ((level + N_LEVEL - 1) % N_LEVEL, seq)
     end = ((z == 0) & (x_hi == 0)) | ((z == N_Z - 1) & (x_hi == 1))
     passes = jnp.logical_not(((z == 0) & (x_hi == 1)) | ((z == N_Z - 1) & (x_hi == 0)))
@@ -64,20 +65,18 @@
     greet(across)
     greet(sibling)
 
-    @pl.when(jnp.logical_not(end))
-    def _():
-        greet(along_from)
-
-    greet(on_level(1 - x_lo, 0))
-
-    @pl.when(y < RELAYED)
+    @pl.when(z < N_Z - 1)
+    def _():
+        greet(at(z + 1, x_hi, core))
+
+    @pl.when(y < N_Y - 1)
     def _():
         greet(on_level(x_lo, y + 1))
 
-    @pl.when(y == RELAYED)
-    def _():
-        for row in range(RELAYED):
-            greet(on_level(x_lo, row))
+    @pl.when(y == 0)
+    def _():
+        for row in range(N_Y):
+            greet(on_level(1 - x_lo, row))
 
     def load_gate():
         return pltpu.make_async_copy(gate_hbm, gate_table, sem_gate)
@@ -145,11 +144,18 @@
         for kind in range(2):
             load_own(h, kind).start()
     load_gate().start()
-    count = 2 + passes.astype(jnp.int32) + 1 + (y < RELAYED).astype(jnp.int32)
-    count = count + RELAYED * (y == 0).astype(jnp.int32)
-    pl.semaphore_wait(barrier, count)
+    pl.semaphore_wait(barrier, 3 + (z > 0).astype(jnp.int32) + (y > 0).astype(jnp.int32))
     for h in range(WINDOW):
         send_own(h)
+    @pl.when((x_hi == 0) & (z > 0))
+    def _():
+        pl.semaphore_signal(
+            along_ready, inc=1, device_id=at(z - 1, x_hi, core), device_id_type=MESH
+        )
+
+    pl.semaphore_signal(
+        level_ready, inc=1, device_id=on_level(1 - x_lo, 0), device_id_type=MESH
+    )
     for h in range(WINDOW):
         load_rest(h)
 
@@ -205,24 +211,26 @@
         )
 
     def step(t, carry):
-        for kind in range(2):
-
-            @pl.when(t < HEADS)
-            def _():
-                u = 2 * t + kind
-                to_across(t, kind).wait_recv()
-
-                @pl.when(passes)
-                def _():
-                    to_along(u).start()
-
-                @pl.when(shares_across)
-                def _():
-                    share(ACROSS, u).start()
-
-            @pl.when((t >= 1) & (t <= HEADS))
-            def _():
-                u = 2 * t - 2 + kind
+        def arrived(kind):
+            u = 2 * t + kind
+            to_across(t, kind).wait_recv()
+
+            @pl.when(passes)
+            def _():
+                to_along(u).start()
+
+            @pl.when(shares_across)
+            def _():
+                share(ACROSS, u).start()
+
+        @pl.when(t < HEADS)
+        def _():
+            arrived(0)
+
+        @pl.when((t >= LAG_PASS) & (t < HEADS + LAG_PASS))
+        def _():
+            for kind in range(2):
+                u = 2 * (t - LAG_PASS) + kind
 
                 @pl.when(end)
                 def _():
@@ -233,6 +241,10 @@
                 @pl.when(jnp.logical_not(shares_across))
                 def _():
                     share(ALONG, u).start()
+
+        @pl.when(t < HEADS)
+        def _():
+            arrived(1)
 
         @pl.when(t + WINDOW < HEADS)
         def _():
@@ -249,6 +261,10 @@
             load_s(h).wait()
             compute(h)
 
+            @pl.when((y == 0) & (h == 0))
+            def _():
+                pl.semaphore_wait(level_ready, N_Y)
+
             @pl.when((y == 0) & (h < RELAYED))
             def _():
                 to_relay(h).start()
@@ -265,6 +281,10 @@
             from_relay().start()
 
         return carry
+
+    @pl.when((x_hi == 0) & (z < N_Z - 1))
+    def _():
+        pl.semaphore_wait(along_ready, 1)
 
     lax.fori_loop(0, HEADS + LAG_COMPUTE, step, 0)
 
@@ -289,6 +309,19 @@
     @pl.when(y < RELAYED)
     def _():
         from_relay().wait_send()
+
+
+def write_out(vel_from, adv_from, vel_to, adv_to, sems):
+    rows = TOK // PIECES
+    moves = []
+    for i, (source, target) in enumerate(((vel_from, vel_to), (adv_from, adv_to))):
+        for j in range(PIECES):
+            part = pl.ds(j * rows, rows)
+            moves.append(pltpu.make_async_copy(source.at[part], target.at[part], sems.at[i, j]))
+    for move in moves:
+        move.start()
+    for move in moves:
+        move.wait()
 
 
 def on_device(queries, keys, values, state, timestep, gate_table):
@@ -316,12 +349,22 @@
         ]
         + [pltpu.SemaphoreType.DMA((2 * HEADS,))] * 9
         + [pltpu.SemaphoreType.DMA((HEADS,))] * 5
-        + [pltpu.SemaphoreType.DMA] * 3,
+        + [pltpu.SemaphoreType.DMA] * 3
+        + [pltpu.SemaphoreType.REGULAR] * 2,
         compiler_params=pltpu.CompilerParams(
-            collective_id=0, has_side_effects=True, vmem_limit_bytes=60 << 20
+            collective_id=0, has_side_effects=True, vmem_limit_bytes=32 << 20
         ),
         name="window_attention",
-    )(timestep, gate_table, queries[0], keys[0], values[0], state[0])
+    )(timestep, *[pltpu.with_memory_space_constraint(a, pltpu.HBM) for a in (gate_table, queries[0], keys[0], values[0], state[0])])
+    velocity, advanced = pl.pallas_call(
+        write_out,
+        out_shape=(block, block),
+        in_specs=[pl.BlockSpec(memory_space=pltpu.VMEM)] * 2,
+        out_specs=(anywhere, anywhere),
+        scratch_shapes=[pltpu.SemaphoreType.DMA((2, PIECES))],
+        compiler_params=pltpu.CompilerParams(vmem_limit_bytes=16 << 20),
+        name="write_out",
+    )(velocity, advanced)
     return (velocity[None], advanced[None])
 
 

time: 66.6 us -> 58.5 us (0.88)
  the two profiles are of different devices: /device:TPU:61 before, /device:TPU:223 now
where the time goes in v3:
time: 58.5 us; the launch traced here: 58.3 us
  Pallas kernels  57 us (97%)
  between operations  1.29 us (2%)
    pallas_call x1, Pallas kernels, on_device(): pl.pallas_call(kernel, out_shape=(block, block), in_specs=[pl.BlockSpec(m...  55.9 us
    pallas_call x1, Pallas kernels, on_device(): pl.pallas_call(write_out, out_shape=(block, block), in_specs=[pl.BlockSpe...  1.17 us

profile of v3, /device:TPU:223, one launch (start us, length us, event | category | flops | bytes accessed | tf_op | source)
XLA Modules:
  0.0 58.3 jit_solution(7231831316792730870)
XLA Ops:
  1.3 55.9 %window_attention.1 = (bf16[256,1536]{1,0:T(8,128)(2,1)S(1)}, bf16[256,1536]{1,0:T(8,128)(2,1)S(1)}) custom-call(s32[1]{0:T(128)S(6)} %copy.8.ts_ref, bf16[16,1536]{1,0:T(8,128)(2,1)} %gate_hbm.1, bf16[256,1536]{1,0:T(8,128)(2,1)} %bitcast.6, bf16[256,1536]{1,0:T(8,128)(2,1)} %bitcast.7, bf16[256,1536]{1,0:T(8,128)(2,1)} %bitcast.8, bf16[256,1536]{1,0:T(8,128)(2,1)} %bitcast.9), custom_call_target="tpu_custom_call" | custom-call | tf_op jit(solution)/shard_map/window_attention/pallas_call | solution.py:332
  57.1 1.2 %write_out.1 = (bf16[256,1536]{1,0:T(8,128)(2,1)}, bf16[256,1536]{1,0:T(8,128)(2,1)}) custom-call(bf16[256,1536]{1,0:T(8,128)(2,1)S(1)} %get-tuple-element.6.vel_from, bf16[256,1536]{1,0:T(8,128)(2,1)S(1)} %get-tuple-element.7.adv_from), custom_call_target="tpu_custom_call" | custom-call | tf_op jit(solution)/shard_map/write_out/pallas_call | solution.py:359

commit v4 on v3

--- a/solution.py
+++ b/solution.py
@@ -19,7 +19,10 @@
 LAG_PASS = 2
 LAG_COMPUTE = 2
 LAG_RELAY = 3
-RELAYED = N_Y - 1
+ROWS = (5, 6, 0, 1, 2, 3, 0)
+SLOTS = (0, 0, 0, 0, 0, 0, 1)
+RELAYED = len(ROWS)
+KEPT = 4
 MESH = pl.DeviceIdType.MESH
 OWN, SIB, ACROSS, ALONG, SHARED = range(5)
 FLOOR_VALUE = -1e30
@@ -31,7 +34,7 @@
 
 def kernel(
     ts_ref, gate_hbm, q_hbm, k_hbm, v_hbm, s_hbm, vel_hbm, adv_hbm,
-    kv, qs, ss, vel, upd, gate_table, gates, relay,
+    kv, tops, totals, sums, qs, ss, upd, vel, gate_table, gates, relay,
     sem_own, send_sib, recv_sib, send_x, recv_x, send_z, recv_z, send_d, recv_d,
     sem_q, sem_s, sem_vel, send_l, recv_l, sem_gate, send_r, recv_r, along_ready, level_ready,
 ):
@@ -123,10 +126,16 @@
         return remote(upd.at[h], columns(adv_hbm, h), send_l.at[h], recv_l.at[h], level_to)
 
     def to_relay(h):
-        return remote(upd.at[h], relay, send_l.at[h], recv_r, on_level(1 - x_lo, h))
-
-    def from_relay():
-        return remote(relay, columns(adv_hbm, y), send_r, recv_l.at[y], on_level(x_lo, RELAYED))
+        return remote(
+            upd.at[h], relay.at[SLOTS[h]], send_l.at[h], recv_r.at[SLOTS[h]],
+            on_level(1 - x_lo, ROWS[h]),
+        )
+
+    def from_relay(h):
+        return remote(
+            relay.at[SLOTS[h]], columns(adv_hbm, h), send_r.at[SLOTS[h]], recv_l.at[h],
+            on_level(x_lo, N_Y - 1),
+        )
 
     def send_own(h):
         for kind in range(2):
@@ -173,37 +182,58 @@
     bias_shared = jnp.where(end & shares_across, FLOOR_VALUE, 0.0)
     scaling = math.log2(math.e) / math.sqrt(HEAD_DIM)
 
-    def compute(h):
-        query = qs[h]
-        scores = []
-        for slot in range(5):
-            part = (
-                lax.dot_general(
-                    query, kv[slot, 2 * h], (((1,), (1,)), ((), ())),
-                    preferred_element_type=jnp.float32,
-                )
-                * scaling
+    def score(h, slot):
+        part = (
+            lax.dot_general(
+                qs[h], kv[slot, 2 * h], (((1,), (1,)), ((), ())),
+                preferred_element_type=jnp.float32,
             )
-            if slot == ALONG:
-                part = part + bias_along
-            if slot == SHARED:
-                part = part + bias_shared
-            scores.append(part)
-        top = scores[0]
-        for part in scores[1:]:
-            top = jnp.maximum(top, part)
-        top = jnp.max(top, axis=-1, keepdims=True)
+            * scaling
+        )
+        if slot == ALONG:
+            part = part + bias_along
+        if slot == SHARED:
+            part = part + bias_shared
+        return part
+
+    def weigh(h, slots, scores, top):
         total = None
         blended = None
-        for slot in range(5):
-            weights = jnp.exp2(scores[slot] - top)
+        for slot, part in zip(slots, scores):
+            weights = jnp.exp2(part - top)
             total = weights if total is None else total + weights
             product = jnp.dot(
                 weights.astype(jnp.bfloat16), kv[slot, 2 * h + 1],
                 preferred_element_type=jnp.float32,
             )
             blended = product if blended is None else blended + product
-        attended = blended / jnp.sum(total, axis=-1, keepdims=True)
+        return jnp.sum(total, axis=-1, keepdims=True), blended
+
+    def highest(scores):
+        top = scores[0]
+        for part in scores[1:]:
+            top = jnp.maximum(top, part)
+        return jnp.max(top, axis=-1, keepdims=True)
+
+    FIRST, REST = (OWN, SIB, ACROSS), (ALONG, SHARED)
+
+    def compute_first(h):
+        place = lax.rem(h, KEPT)
+        scores = [score(h, slot) for slot in FIRST]
+        top = highest(scores)
+        total, blended = weigh(h, FIRST, scores, top)
+        tops[place] = top
+        totals[place] = total
+        sums[place] = blended
+
+    def compute_rest(h):
+        place = lax.rem(h, KEPT)
+        scores = [score(h, slot) for slot in REST]
+        top = jnp.maximum(highest(scores), tops[place])
+        total, blended = weigh(h, REST, scores, top)
+        kept = jnp.exp2(tops[place] - top)
+        total = total + totals[place] * kept
+        attended = (blended + sums[place] * kept) / total
         velocity = (gates[h][0:1] * attended).astype(jnp.bfloat16)
         vel[h] = velocity
         upd[h] = (ss[h].astype(jnp.float32) + factor * velocity.astype(jnp.float32)).astype(
@@ -255,19 +285,19 @@
         def _():
             h = t - LAG_COMPUTE
             for kind in range(2):
-                to_sibling(h, kind).wait_recv()
                 share(ACROSS, 2 * h + kind).wait_recv()
-            load_q(h).wait()
             load_s(h).wait()
-            compute(h)
+            compute_rest(h)
 
             @pl.when((y == 0) & (h == 0))
             def _():
                 pl.semaphore_wait(level_ready, N_Y)
 
-            @pl.when((y == 0) & (h < RELAYED))
-            def _():
-                to_relay(h).start()
+            for i in range(RELAYED):
+
+                @pl.when((y == 0) & (h == i))
+                def _():
+                    to_relay(i).start()
 
             @pl.when((y > 0) | (h >= RELAYED))
             def _():
@@ -275,10 +305,19 @@
 
             store_vel(h).start()
 
-        @pl.when((y < RELAYED) & (t == y + LAG_COMPUTE + LAG_RELAY))
-        def _():
-            to_relay(y).wait_recv()
-            from_relay().start()
+        @pl.when(t < HEADS)
+        def _():
+            for kind in range(2):
+                to_sibling(t, kind).wait_recv()
+            load_q(t).wait()
+            compute_first(t)
+
+        for i in range(RELAYED):
+
+            @pl.when((y == ROWS[i]) & (t == i + LAG_COMPUTE + LAG_RELAY))
+            def _():
+                to_relay(i).wait_recv()
+                from_relay(i).start()
 
         return carry
 
@@ -306,9 +345,11 @@
 
     lax.fori_loop(0, HEADS, drain, 0)
 
-    @pl.when(y < RELAYED)
-    def _():
-        from_relay().wait_send()
+    for i in range(RELAYED):
+
+        @pl.when(y == ROWS[i])
+        def _():
+            from_relay(i).wait_send()
 
 
 def write_out(vel_from, adv_from, vel_to, adv_to, sems):
@@ -339,17 +380,21 @@
         out_specs=(anywhere, anywhere),
         scratch_shapes=[
             pltpu.VMEM((5, 2 * HEADS, TOK, HEAD_DIM), jnp.bfloat16),
+            pltpu.VMEM((KEPT, TOK, 1), jnp.float32),
+            pltpu.VMEM((KEPT, TOK, 1), jnp.float32),
+            pltpu.VMEM((KEPT, TOK, HEAD_DIM), jnp.float32),
             pltpu.VMEM(heads, jnp.bfloat16),
             pltpu.VMEM(heads, jnp.bfloat16),
             pltpu.VMEM(heads, jnp.bfloat16),
             pltpu.VMEM(heads, jnp.bfloat16),
             pltpu.VMEM((STEPS, width), jnp.bfloat16),
             pltpu.VMEM((HEADS, 8, HEAD_DIM), jnp.float32),
-            pltpu.VMEM((TOK, HEAD_DIM), jnp.bfloat16),
+            pltpu.VMEM((2, TOK, HEAD_DIM), jnp.bfloat16),
         ]
         + [pltpu.SemaphoreType.DMA((2 * HEADS,))] * 9
         + [pltpu.SemaphoreType.DMA((HEADS,))] * 5
-        + [pltpu.SemaphoreType.DMA] * 3
+        + [pltpu.SemaphoreType.DMA]
+        + [pltpu.SemaphoreType.DMA((2,))] * 2
         + [pltpu.SemaphoreType.REGULAR] * 2,
         compiler_params=pltpu.CompilerParams(
             collective_id=0, has_side_effects=True, vmem_limit_bytes=32 << 20

time: 58.5 us -> 57.3 us (0.979)
  the two profiles are of different devices: /device:TPU:223 before, /device:TPU:63 now
where the time goes in v4:
time: 57.3 us; the launch traced here: 57.1 us
  Pallas kernels  55.8 us (97%)
  between operations  1.29 us (2%)
    pallas_call x1, Pallas kernels, on_device(): pl.pallas_call(kernel, out_shape=(block, block), in_specs=[pl.BlockSpec(m...  54.7 us
    pallas_call x1, Pallas kernels, on_device(): pl.pallas_call(write_out, out_shape=(block, block), in_specs=[pl.BlockSpe...  1.17 us

profile of v4, /device:TPU:63, one launch (start us, length us, event | category | flops | bytes accessed | tf_op | source)
XLA Modules:
  0.0 57.1 jit_solution(12084057798760753169)
XLA Ops:
  1.3 54.7 %window_attention.1 = (bf16[256,1536]{1,0:T(8,128)(2,1)S(1)}, bf16[256,1536]{1,0:T(8,128)(2,1)S(1)}) custom-call(s32[1]{0:T(128)S(6)} %copy.8.ts_ref, bf16[16,1536]{1,0:T(8,128)(2,1)} %gate_hbm.1, bf16[256,1536]{1,0:T(8,128)(2,1)} %bitcast.6, bf16[256,1536]{1,0:T(8,128)(2,1)} %bitcast.7, bf16[256,1536]{1,0:T(8,128)(2,1)} %bitcast.8, bf16[256,1536]{1,0:T(8,128)(2,1)} %bitcast.9), custom_call_target="tpu_custom_call" | custom-call | tf_op jit(solution)/shard_map/window_attention/pallas_call | solution.py:373
  55.9 1.2 %write_out.1 = (bf16[256,1536]{1,0:T(8,128)(2,1)}, bf16[256,1536]{1,0:T(8,128)(2,1)}) custom-call(bf16[256,1536]{1,0:T(8,128)(2,1)S(1)} %get-tuple-element.6.vel_from, bf16[256,1536]{1,0:T(8,128)(2,1)S(1)} %get-tuple-element.7.adv_from), custom_call_target="tpu_custom_call" | custom-call | tf_op jit(solution)/shard_map/write_out/pallas_call | solution.py:404

commit v5 on v4

--- a/solution.py
+++ b/solution.py
@@ -98,42 +98,44 @@
         return pltpu.make_async_copy(columns(s_hbm, h), ss.at[h], sem_s.at[h])
 
     def store_vel(h):
-        return pltpu.make_async_copy(vel.at[h], columns(vel_hbm, h), sem_vel.at[h])
+        return pltpu.make_async_copy(vel.at[h], columns(vel_hbm, h), sem_vel)
 
     def remote(source, target, send, recv, device):
         return pltpu.make_async_remote_copy(
             source, target, send, recv, device_id=device, device_id_type=MESH
         )
 
-    def to_sibling(h, kind):
-        u = 2 * h + kind
-        return remote(kv.at[OWN, u], kv.at[SIB, u], send_sib.at[u], recv_sib.at[u], sibling)
+    def to_sibling(h):
+        both = pl.ds(2 * h, 2)
+        return remote(
+            kv.at[OWN, both], kv.at[SIB, both], send_sib, recv_sib.at[h], sibling
+        )
 
     def to_across(h, kind):
         u = 2 * h + kind
-        return remote(kv.at[OWN, u], kv.at[ACROSS, u], send_x.at[u], recv_x.at[u], across)
+        return remote(kv.at[OWN, u], kv.at[ACROSS, u], send_x, recv_x.at[u], across)
 
     def to_along(u):
-        return remote(kv.at[ACROSS, u], kv.at[ALONG, u], send_z.at[u], recv_z.at[u], along_to)
+        return remote(kv.at[ACROSS, u], kv.at[ALONG, u], send_z, recv_z.at[u], along_to)
 
     def own_as_along(u):
         return pltpu.make_async_copy(kv.at[OWN, u], kv.at[ALONG, u], recv_z.at[u])
 
     def share(slot, u):
-        return remote(kv.at[slot, u], kv.at[SHARED, u], send_d.at[u], recv_d.at[u], sibling)
+        return remote(kv.at[slot, u], kv.at[SHARED, u], send_d, recv_d.at[u], sibling)
 
     def to_level(h):
-        return remote(upd.at[h], columns(adv_hbm, h), send_l.at[h], recv_l.at[h], level_to)
+        return remote(upd.at[h], columns(adv_hbm, h), send_l, recv_l, level_to)
 
     def to_relay(h):
         return remote(
-            upd.at[h], relay.at[SLOTS[h]], send_l.at[h], recv_r.at[SLOTS[h]],
+            upd.at[h], relay.at[SLOTS[h]], send_l, recv_r.at[SLOTS[h]],
             on_level(1 - x_lo, ROWS[h]),
         )
 
     def from_relay(h):
         return remote(
-            relay.at[SLOTS[h]], columns(adv_hbm, h), send_r.at[SLOTS[h]], recv_l.at[h],
+            relay.at[SLOTS[h]], columns(adv_hbm, h), send_r.at[SLOTS[h]], recv_l,
             on_level(x_lo, N_Y - 1),
         )
 
@@ -142,8 +144,7 @@
             load_own(h, kind).wait()
         for kind in range(2):
             to_across(h, kind).start()
-        for kind in range(2):
-            to_sibling(h, kind).start()
+        to_sibling(h).start()
 
     def load_rest(h):
         load_q(h).start()
@@ -165,7 +166,7 @@
     pl.semaphore_signal(
         level_ready, inc=1, device_id=on_level(1 - x_lo, 0), device_id_type=MESH
     )
-    for h in range(WINDOW):
+    for h in range(HEADS):
         load_rest(h)
 
     load_gate().wait()
@@ -279,7 +280,6 @@
         @pl.when(t + WINDOW < HEADS)
         def _():
             send_own(t + WINDOW)
-            load_rest(t + WINDOW)
 
         @pl.when(t >= LAG_COMPUTE)
         def _():
@@ -307,8 +307,7 @@
 
         @pl.when(t < HEADS)
         def _():
-            for kind in range(2):
-                to_sibling(t, kind).wait_recv()
+            to_sibling(t).wait_recv()
             load_q(t).wait()
             compute_first(t)
 
@@ -327,23 +326,17 @@
 
     lax.fori_loop(0, HEADS + LAG_COMPUTE, step, 0)
 
-    def drain(h, carry):
-        for kind in range(2):
-            u = 2 * h + kind
-            to_sibling(h, kind).wait_send()
-            to_across(h, kind).wait_send()
-
-            @pl.when(passes)
-            def _():
-                to_along(u).wait_send()
-
-            share(ACROSS, u).wait_send()
-        store_vel(h).wait()
-        to_level(h).wait_send()
-        to_level(h).wait_recv()
-        return carry
-
-    lax.fori_loop(0, HEADS, drain, 0)
+    remote(kv.at[OWN], kv.at[SIB], send_sib, recv_sib.at[0], sibling).wait_send()
+    remote(kv.at[OWN], kv.at[ACROSS], send_x, recv_x.at[0], across).wait_send()
+    remote(kv.at[ACROSS], kv.at[SHARED], send_d, recv_d.at[0], sibling).wait_send()
+    remote(upd, upd, send_l, recv_l, level_to).wait_send()
+
+    @pl.when(passes)
+    def _():
+        remote(kv.at[ACROSS], kv.at[ALONG], send_z, recv_z.at[0], along_to).wait_send()
+
+    pltpu.make_async_copy(vel_hbm, vel_hbm, sem_vel).wait()
+    remote(adv_hbm, adv_hbm, send_l, recv_l, level_to).wait_recv()
 
     for i in range(RELAYED):
 
@@ -391,8 +384,10 @@
             pltpu.VMEM((HEADS, 8, HEAD_DIM), jnp.float32),
             pltpu.VMEM((2, TOK, HEAD_DIM), jnp.bfloat16),
         ]
-        + [pltpu.SemaphoreType.DMA((2 * HEADS,))] * 9
-        + [pltpu.SemaphoreType.DMA((HEADS,))] * 5
+        + [pltpu.SemaphoreType.DMA((2 * HEADS,))]
+        + [pltpu.SemaphoreType.DMA, pltpu.SemaphoreType.DMA((2 * HEADS,))] * 4
+        + [pltpu.SemaphoreType.DMA((HEADS,))] * 2
+        + [pltpu.SemaphoreType.DMA] * 3
         + [pltpu.SemaphoreType.DMA]
         + [pltpu.SemaphoreType.DMA((2,))] * 2
         + [pltpu.SemaphoreType.REGULAR] * 2,

time: 57.3 us -> 56.2 us (0.981)
  Pallas kernels: 55.8 us -> 54.7 us
    pallas_call x1, Pallas kernels: 54.7 us -> 53.5 us  [on_device(): pl.pallas_call(kernel, out_shape=(block, block), in_specs=[pl.BlockSpec(m...]
where the time goes in v5:
time: 56.2 us; the launch traced here: 56 us
  Pallas kernels  54.7 us (97%)
  between operations  1.29 us (2%)
    pallas_call x1, Pallas kernels, on_device(): pl.pallas_call(kernel, out_shape=(block, block), in_specs=[pl.BlockSpec(m...  53.5 us
    pallas_call x1, Pallas kernels, on_device(): pl.pallas_call(write_out, out_shape=(block, block), in_specs=[pl.BlockSpe...  1.17 us

profile of v5, /device:TPU:63, one launch (start us, length us, event | category | flops | bytes accessed | tf_op | source)
XLA Modules:
  0.0 56.0 jit_solution(10268541136656214702)
XLA Ops:
  1.3 53.5 %window_attention.1 = (bf16[256,1536]{1,0:T(8,128)(2,1)S(1)}, bf16[256,1536]{1,0:T(8,128)(2,1)S(1)}) custom-call(s32[1]{0:T(128)S(6)} %copy.8.ts_ref, bf16[16,1536]{1,0:T(8,128)(2,1)} %gate_hbm.1, bf16[256,1536]{1,0:T(8,128)(2,1)} %bitcast.6, bf16[256,1536]{1,0:T(8,128)(2,1)} %bitcast.7, bf16[256,1536]{1,0:T(8,128)(2,1)} %bitcast.8, bf16[256,1536]{1,0:T(8,128)(2,1)} %bitcast.9), custom_call_target="tpu_custom_call" | custom-call | tf_op jit(solution)/shard_map/window_attention/pallas_call | solution.py:366
  54.8 1.2 %write_out.1 = (bf16[256,1536]{1,0:T(8,128)(2,1)}, bf16[256,1536]{1,0:T(8,128)(2,1)}) custom-call(bf16[256,1536]{1,0:T(8,128)(2,1)S(1)} %get-tuple-element.6.vel_from, bf16[256,1536]{1,0:T(8,128)(2,1)S(1)} %get-tuple-element.7.adv_from), custom_call_target="tpu_custom_call" | custom-call | tf_op jit(solution)/shard_map/write_out/pallas_call | solution.py:399

commit v6 on v5

--- a/solution.py
+++ b/solution.py
@@ -127,6 +127,11 @@
     def to_level(h):
         return remote(upd.at[h], columns(adv_hbm, h), send_l, recv_l, level_to)
 
+    def part_to_level(h, rows):
+        return remote(
+            upd.at[h, rows], columns(adv_hbm.at[rows], h), send_l, recv_l, level_to
+        )
+
     def to_relay(h):
         return remote(
             upd.at[h], relay.at[SLOTS[h]], send_l, recv_r.at[SLOTS[h]],
@@ -183,10 +188,10 @@
     bias_shared = jnp.where(end & shares_across, FLOOR_VALUE, 0.0)
     scaling = math.log2(math.e) / math.sqrt(HEAD_DIM)
 
-    def score(h, slot):
+    def score(h, slot, rows):
         part = (
             lax.dot_general(
-                qs[h], kv[slot, 2 * h], (((1,), (1,)), ((), ())),
+                qs[h, rows], kv[slot, 2 * h], (((1,), (1,)), ((), ())),
                 preferred_element_type=jnp.float32,
             )
             * scaling
@@ -220,26 +225,27 @@
 
     def compute_first(h):
         place = lax.rem(h, KEPT)
-        scores = [score(h, slot) for slot in FIRST]
+        scores = [score(h, slot, pl.ds(0, TOK)) for slot in FIRST]
         top = highest(scores)
         total, blended = weigh(h, FIRST, scores, top)
         tops[place] = top
         totals[place] = total
         sums[place] = blended
 
-    def compute_rest(h):
+    def compute_rest(h, rows):
         place = lax.rem(h, KEPT)
-        scores = [score(h, slot) for slot in REST]
-        top = jnp.maximum(highest(scores), tops[place])
+        scores = [score(h, slot, rows) for slot in REST]
+        earlier = tops[place, rows]
+        top = jnp.maximum(highest(scores), earlier)
         total, blended = weigh(h, REST, scores, top)
-        kept = jnp.exp2(tops[place] - top)
-        total = total + totals[place] * kept
-        attended = (blended + sums[place] * kept) / total
+        kept = jnp.exp2(earlier - top)
+        total = total + totals[place, rows] * kept
+        attended = (blended + sums[place, rows] * kept) / total
         velocity = (gates[h][0:1] * attended).astype(jnp.bfloat16)
-        vel[h] = velocity
-        upd[h] = (ss[h].astype(jnp.float32) + factor * velocity.astype(jnp.float32)).astype(
-            jnp.bfloat16
-        )
+        vel[h, rows] = velocity
+        upd[h, rows] = (
+            ss[h, rows].astype(jnp.float32) + factor * velocity.astype(jnp.float32)
+        ).astype(jnp.bfloat16)
 
     def step(t, carry):
         def arrived(kind):
@@ -287,7 +293,17 @@
             for kind in range(2):
                 share(ACROSS, 2 * h + kind).wait_recv()
             load_s(h).wait()
-            compute_rest(h)
+
+            @pl.when(h < HEADS - 1)
+            def _():
+                compute_rest(h, pl.ds(0, TOK))
+
+            @pl.when(h == HEADS - 1)
+            def _():
+                for half in range(2):
+                    rows = pl.ds(half * (TOK // 2), TOK // 2)
+                    compute_rest(h, rows)
+                    part_to_level(h, rows).start()
 
             @pl.when((y == 0) & (h == 0))
             def _():
@@ -299,7 +315,7 @@
                 def _():
                     to_relay(i).start()
 
-            @pl.when((y > 0) | (h >= RELAYED))
+            @pl.when(((y > 0) | (h >= RELAYED)) & (h < HEADS - 1))
             def _():
                 to_level(h).start()
 

time: 56.2 us -> 56.1 us (level)
  no operation moved by 1% of the time
where the time goes in v6:
time: 56.1 us; the launch traced here: 55.9 us
  Pallas kernels  54.6 us (97%)
  between operations  1.29 us (2%)
    pallas_call x1, Pallas kernels, on_device(): pl.pallas_call(kernel, out_shape=(block, block), in_specs=[pl.BlockSpec(m...  53.4 us
    pallas_call x1, Pallas kernels, on_device(): pl.pallas_call(write_out, out_shape=(block, block), in_specs=[pl.BlockSpe...  1.17 us

profile of v6, /device:TPU:63, one launch (start us, length us, event | category | flops | bytes accessed | tf_op | source)
XLA Modules:
  0.0 55.9 jit_solution(10757369110068492460)
XLA Ops:
  1.3 53.4 %window_attention.1 = (bf16[256,1536]{1,0:T(8,128)(2,1)S(1)}, bf16[256,1536]{1,0:T(8,128)(2,1)S(1)}) custom-call(s32[1]{0:T(128)S(6)} %copy.8.ts_ref, bf16[16,1536]{1,0:T(8,128)(2,1)} %gate_hbm.1, bf16[256,1536]{1,0:T(8,128)(2,1)} %bitcast.6, bf16[256,1536]{1,0:T(8,128)(2,1)} %bitcast.7, bf16[256,1536]{1,0:T(8,128)(2,1)} %bitcast.8, bf16[256,1536]{1,0:T(8,128)(2,1)} %bitcast.9), custom_call_target="tpu_custom_call" | custom-call | tf_op jit(solution)/shard_map/window_attention/pallas_call | solution.py:382
  54.7 1.2 %write_out.1 = (bf16[256,1536]{1,0:T(8,128)(2,1)}, bf16[256,1536]{1,0:T(8,128)(2,1)}) custom-call(bf16[256,1536]{1,0:T(8,128)(2,1)S(1)} %get-tuple-element.6.vel_from, bf16[256,1536]{1,0:T(8,128)(2,1)S(1)} %get-tuple-element.7.adv_from), custom_call_target="tpu_custom_call" | custom-call | tf_op jit(solution)/shard_map/write_out/pallas_call | solution.py:415
